TPU v7x, 128 devices: a whole 4x4x4 slice. The times are simulated.
128 devices in a mesh: user: 8 (over z_hi, x), cand: 8 (over z_lo, y), tensor: 2 (over core).
Axes of the slice: x: 4, y: 4, z: 4 (z_hi: 2, z_lo: 2; z = z_hi * 2 + z_lo), core: 2. Of those that a mesh axis runs over, the one named last changes fastest.
Arguments:
- cand_embed: bfloat16 [8, 4096, 1024], P('user', 'cand'), may hold values from -6 to 6
- cand_ids: int32 [8, 4096], P('user', 'cand'), may hold values from 0 to 255
- hist_ids: int32 [8, 4096], P('user', ('cand', 'tensor')), may hold values from 0 to 255
- hist_len: int32 [8], P('user'), may hold values from 1 to 4096, as said below
- hist_keys: bfloat16 [8, 2, 4096, 1024], P('user', None, ('cand', 'tensor')), may hold values from -6 to 6
- hist_values: bfloat16 [8, 2, 4096, 1024], P('user', None, ('cand', 'tensor')), may hold values from -6 to 6
- w_in: bfloat16 [2, 1024, 4, 1024], P(None, None, None, 'tensor'), may hold values from -0.1875 to 0.1875
- w_out: bfloat16 [2, 1024, 1024], P(None, 'tensor'), may hold values from -0.1875 to 0.1875
Outputs:
- cand_out: float32 [8, 4096, 1024], P('user', 'cand')
Inputs may be any that keep to these rules, and one draw needn't show every extreme that they name: `hist_len`: some user has exactly 4096 live history positions.
All inputs are finite; a program needn't handle non-finite values.
Results may differ from a plain program's by a relative error of at most 0.017.
Values may be sent and summed in bfloat16 or wider, within the bound.
A program may use at most 128 MiB of HBM per device.

v0:
```python
import jax
import jax.numpy as jnp
from jax import lax
from jax.sharding import PartitionSpec as P

HEADS = 8
LAYERS = 2


def row_norm(values):
    return values * lax.rsqrt(jnp.mean(values * values, axis=-1, keepdims=True) + 1e-06)


def on_device(cand_embed, cand_ids, hist_ids, hist_len, hist_keys, hist_values, w_in, w_out):
    tensor_pos = lax.axis_index("tensor")
    width = cand_embed.shape[2]
    local = w_in.shape[3]
    head_dim = width // HEADS
    heads_here = local // head_dim
    scale = head_dim ** (-0.5)
    count = cand_embed.shape[1]
    state = cand_embed[0].astype(jnp.float32)
    cand_item = cand_ids[0]
    length = hist_len[0]
    column = tensor_pos * local
    normed = row_norm(state).astype(jnp.bfloat16)
    for layer in range(LAYERS):
        proj = jax.nn.silu(
            jnp.dot(
                normed, w_in[layer].reshape(width, 4 * local), preferred_element_type=jnp.float32
            )
        )
        proj = proj.reshape(count, 4, local)
        gate_u = proj[:, 0]
        value_b = proj[:, 1].astype(jnp.bfloat16)
        query_b = proj[:, 2].astype(jnp.bfloat16)
        key_b = proj[:, 3].astype(jnp.bfloat16)
        query_h = query_b.reshape(count, heads_here, head_dim).transpose(1, 0, 2)
        empty = jnp.zeros((heads_here, count, head_dim), jnp.float32)
        keys = lax.all_gather(hist_keys[0, layer], ("cand", "tensor"), axis=0, tiled=True)
        values = lax.all_gather(hist_values[0, layer], ("cand", "tensor"), axis=0, tiled=True)
        items = lax.all_gather(hist_ids[0], ("cand", "tensor"), axis=0, tiled=True)
        rows = keys.shape[0]
        keys = lax.dynamic_slice_in_dim(keys, column, local, 1)
        values = lax.dynamic_slice_in_dim(values, column, local, 1)

        def compute(total):
            key_h = keys.reshape(rows, heads_here, head_dim).transpose(1, 0, 2)
            value_h = values.reshape(rows, heads_here, head_dim).transpose(1, 0, 2)
            positions = lax.iota(jnp.int32, rows)
            valid = (positions < length)[None, :] & (items[None, :] != cand_item[:, None])

            def one_head(parts):
                query_one, key_one, value_one = parts
                scores = (
                    jnp.einsum("cd,pd->cp", query_one, key_one, preferred_element_type=jnp.float32)
                    * scale
                )
                weights = jnp.where(valid, jax.nn.silu(scores), 0.0).astype(jnp.bfloat16)
                return jnp.dot(weights, value_one, preferred_element_type=jnp.float32)

            return lax.map(one_head, (query_h, key_h, value_h))

        hist_part = lax.cond(jnp.int32(0) < length, compute, lambda total: total, empty)
        own_scores = (
            jnp.sum(
                query_b.astype(jnp.float32).reshape(count, heads_here, head_dim)
                * key_b.astype(jnp.float32).reshape(count, heads_here, head_dim),
                axis=-1,
            )
            * scale
        )
        own_part = jax.nn.silu(own_scores)[..., None] * value_b.astype(jnp.float32).reshape(
            count, heads_here, head_dim
        )
        attended = (hist_part.transpose(1, 0, 2) + own_part).reshape(count, local)
        product = attended * gate_u
        squares = lax.psum(jnp.sum(product * product, axis=1), "tensor")
        normed_z = (product * lax.rsqrt(squares / width + 1e-06)[:, None]).astype(jnp.bfloat16)
        partial_value = jnp.dot(normed_z, w_out[layer], preferred_element_type=jnp.float32)
        state = state + lax.psum(partial_value.astype(jnp.bfloat16), "tensor").astype(jnp.float32)
        if layer + 1 < LAYERS:
            normed = row_norm(state).astype(jnp.bfloat16)
    return state[None]


def solution(mesh):
    in_specs = (
        P("user", "cand", None),
        P("user", "cand"),
        P("user", ("cand", "tensor")),
        P("user"),
        P("user", None, ("cand", "tensor"), None),
        P("user", None, ("cand", "tensor"), None),
        P(None, None, None, "tensor"),
        P(None, "tensor", None),
    )
    out_specs = P("user", "cand", None)
    return jax.shard_map(
        on_device, mesh=mesh, in_specs=in_specs, out_specs=out_specs, check_vma=False
    )
```

profile of v0, /device:TPU:1, one launch (start us, length us, event | category | flops | bytes accessed | tf_op | source)
XLA Modules:
  0.0 410.3 jit_solution(11231503174238420126)
XLA Ops:
  11.8 7.0 %fusion.62 = (bf16[1,1024,4,512]{3,2,1,0:T(4,128)(2,1)S(1)}, bf16[1,1024,4,512]{3,2,1,0:T(4,128)(2,1)}) fusion(bf16[2,1024,4,512]{3,2,1,0:T(4,128)(2,1)} %param.22), kind=kLoop, calls=%fused_computation.78 | loop fusion | bytes 16777216 | tf_op jit(solution)/shard_map/slice | solution.py:30
  20.5 4.9 %divide_multiply_fusion.1 = f32[512,2048]{1,0:T(8,128)} fusion(bf16[1024,2048]{1,0:T(8,128)(2,1)S(1)} %bitcast.164, bf16[1,512,1024]{2,1,0:T(8,128)(2,1)S(1)} %copy-done, f32[512]{0:T(512)S(1)} %add_rsqrt_fusion.3), kind=kOutput, calls=%fused_computation.37 | convolution fusion | flops 2153250816 | bytes 9439232 | tf_op jit(solution)/shard_map/dot_general | solution.py:29
  25.4 5.4 %copy.25 = f32[512,2048]{0,1:T(8,128)} copy(f32[512,2048]{1,0:T(8,128)} %divide_multiply_fusion.1) | data formatting | bytes 8388608 | tf_op jit(solution)/shard_map/reshape | solution.py:33
  32.1 3.8 convert.15
  36.6 21.6 %all-gather.2 = s32[1,4096]{1,0:T(1,128)S(1)} all-gather(s32[1,256]{1,0:T(1,128)S(1)} %copy-done.5), channel_id=4, replica_groups=mesh['user'=8,'cand'=8,'tensor'=2] {'cand','tensor'}, dimensions={1}, use_global_device_ids=true | all-gather | bytes 17408 | tf_op jit(solution)/shard_map/all_gather | solution.py:42
  60.6 13.5 %all-gather.10.cloned.1.call-done = bf16[1,1,4096,1024]{2,3,1,0:T(8,128)(2,1)} async-done(((bf16[1,1,256,1024]{2,3,1,0:T(8,128)(2,1)}), bf16[1,1,4096,1024]{2,3,1,0:T(8,128)(2,1)}) %all-gather.10.cloned.1.call-update) | async-done | bytes 8388624 | tf_op jit(solution)/shard_map/all_gather | solution.py:40
  74.1 62.4 %all-gather.12.cloned.1.call-done = bf16[1,1,4096,1024]{2,3,1,0:T(8,128)(2,1)} async-done(((bf16[1,1,256,1024]{2,3,1,0:T(8,128)(2,1)}), bf16[1,1,4096,1024]{2,3,1,0:T(8,128)(2,1)}) %all-gather.12.cloned.1.call-update) | async-done | bytes 8388624 | tf_op jit(solution)/shard_map/all_gather | solution.py:41
  136.5 33.8 %conditional.2 = (f32[4,512,128]{2,1,0:T(8,128)}) conditional(s32[]{:T(128)} %convert_element_type.146, () %tuple.33, (bf16[4096,1024]{0,1:T(8,128)(2,1)}, s32[]{:T(128)}, bf16[4096,1024]{0,1:T(8,128)(2,1)}, s32[]{:T(128)}, s32[4096]{0:T(1024)S(1)}, /*index=5*/s32[1,512]{1,0:T(1,128)S(1)}, bf16[4,512,128]{1,2,0:T(8,128)(2,1)S(1)}) %tuple.106), branch_computations={%region_1.2_spmd, %region_2.5_spmd} | conditional | flops 1092620288 | bytes 19296452 | solution.py:64
  136.5 9.4 %constant_dynamic-slice_fusion = (bf16[4096,512]{0,1:T(8,128)(2,1)}, bf16[4096,512]{0,1:T(8,128)(2,1)}) fusion(bf16[4096,1024]{0,1:T(8,128)(2,1)} %get-tuple-element.174, s32[]{:T(128)} %get-tuple-element.170, bf16[4096,1024]{0,1:T(8,128)(2,1)} %get-tuple-element.169), kind=kLoop, calls=%fused_computation.17 | loop fusion | bytes 16777220 | tf_op jit(solution)/shard_map/dynamic_slice | solution.py:45
  146.6 23.7 %while.32 = (s32[]{:T(128)}, f32[4,512,128]{2,1,0:T(8,128)}, bf16[4,512,128]{1,2,0:T(8,128)(2,1)S(1)}, bf16[4,4096,128]{1,2,0:T(8,128)(2,1)}, bf16[4,4096,128]{1...) while((s32[]{:T(128)}, f32[4,512,128]{2,1,0:T(8,128)}, ...), condition=%wide.region_4.4_spmd.clone, body=%wide.region_3.3_spmd.clone.sunk | while | flops 1092616192 | bytes 2515045 | solution.py:62
  146.6 5.9 %fusion.86 = f32[4,512,128]{2,1,0:T(8,128)} fusion(f32[4,512,128]{2,1,0:T(8,128)} %get-tuple-element.446, s32[]{:T(128)S(6)} %copy.49, s32[4096]{0:T(1024)S(1)} %get-tuple-element.460, s32[512]{0:T(512)S(1)} %get-tuple-element.459, pred[4096]{0:T(1024)(128)(4,1)S(1)} %get-tuple-element.461, bf16[4,4096,128]{1,2,0:T(8,128)(2,1)} %get-tuple-element.458, ...), kind=kOutput, calls=%fused_computation.5.clone.1 | convolution fusion | flops 1092616192 | bytes 2514944 | tf_op jit(solution)/shard_map/cond/branch_1_fun/while/body/eval_jaxpr/dot_general | solution.py:60
  152.6 5.9 %fusion.86 = f32[4,512,128]{2,1,0:T(8,128)} fusion(f32[4,512,128]{2,1,0:T(8,128)} %get-tuple-element.446, s32[]{:T(128)S(6)} %copy.49, s32[4096]{0:T(1024)S(1)} %get-tuple-element.460, s32[512]{0:T(512)S(1)} %get-tuple-element.459, pred[4096]{0:T(1024)(128)(4,1)S(1)} %get-tuple-element.461, bf16[4,4096,128]{1,2,0:T(8,128)(2,1)} %get-tuple-element.458, ...), kind=kOutput, calls=%fused_computation.5.clone.1 | convolution fusion | flops 1092616192 | bytes 2514944 | tf_op jit(solution)/shard_map/cond/branch_1_fun/while/body/eval_jaxpr/dot_general | solution.py:60
  158.5 5.9 %fusion.86 = f32[4,512,128]{2,1,0:T(8,128)} fusion(f32[4,512,128]{2,1,0:T(8,128)} %get-tuple-element.446, s32[]{:T(128)S(6)} %copy.49, s32[4096]{0:T(1024)S(1)} %get-tuple-element.460, s32[512]{0:T(512)S(1)} %get-tuple-element.459, pred[4096]{0:T(1024)(128)(4,1)S(1)} %get-tuple-element.461, bf16[4,4096,128]{1,2,0:T(8,128)(2,1)} %get-tuple-element.458, ...), kind=kOutput, calls=%fused_computation.5.clone.1 | convolution fusion | flops 1092616192 | bytes 2514944 | tf_op jit(solution)/shard_map/cond/branch_1_fun/while/body/eval_jaxpr/dot_general | solution.py:60
  164.4 5.9 %fusion.86 = f32[4,512,128]{2,1,0:T(8,128)} fusion(f32[4,512,128]{2,1,0:T(8,128)} %get-tuple-element.446, s32[]{:T(128)S(6)} %copy.49, s32[4096]{0:T(1024)S(1)} %get-tuple-element.460, s32[512]{0:T(512)S(1)} %get-tuple-element.459, pred[4096]{0:T(1024)(128)(4,1)S(1)} %get-tuple-element.461, bf16[4,4096,128]{1,2,0:T(8,128)(2,1)} %get-tuple-element.458, ...), kind=kOutput, calls=%fused_computation.5.clone.1 | convolution fusion | flops 1092616192 | bytes 2514944 | tf_op jit(solution)/shard_map/cond/branch_1_fun/while/body/eval_jaxpr/dot_general | solution.py:60
  173.2 2.5 psum.28
  177.1 3.0 convolution_convert_fusion.1
  182.6 5.6 %copy.38 = bf16[128,8,4,512]{3,1,2,0:T(8,128)(2,1)} copy(bf16[128,8,4,512]{3,2,1,0:T(4,128)(2,1)} %bitcast.149) | data formatting | bytes 8388608
  188.2 17.4 %all-reduce.3.cloned.1.call-done = bf16[512,1024]{1,0:T(8,128)(2,1)} async-done(((bf16[512,1024]{1,0:T(8,128)(2,1)}), bf16[512,1024]{1,0:T(8,128)(2,1)}) %all-reduce.3.cloned.1.call-update) | async-done | bytes 1048592 | tf_op jit(solution)/shard_map/psum | solution.py:81
  207.2 7.3 %divide_multiply_fusion = f32[512,2048]{1,0:T(8,128)} fusion(bf16[1024,2048]{1,0:T(8,128)(2,1)} %bitcast.163, bf16[512,1024]{1,0:T(8,128)(2,1)} %all-reduce.3.cloned.1.call-done, bf16[1,512,1024]{2,1,0:T(8,128)(2,1)S(1)} %copy-done, f32[512]{0:T(512)S(1)} %add_rsqrt_fusion.1), kind=kOutput, calls=%fused_computation.36 | convolution fusion | flops 2154299392 | bytes 10487808 | tf_op jit(solution)/shard_map/dot_general | solution.py:29
  214.5 5.4 %copy.26 = f32[512,2048]{0,1:T(8,128)} copy(f32[512,2048]{1,0:T(8,128)} %divide_multiply_fusion) | data formatting | bytes 8388608 | tf_op jit(solution)/shard_map/reshape | solution.py:33
  224.7 44.4 %all-gather.14.cloned.1.call-done = bf16[1,1,4096,1024]{2,3,1,0:T(8,128)(2,1)} async-done(((bf16[1,1,256,1024]{2,3,1,0:T(8,128)(2,1)}), bf16[1,1,4096,1024]{2,3,1,0:T(8,128)(2,1)}) %all-gather.14.cloned.1.call-update) | async-done | bytes 8388624 | tf_op jit(solution)/shard_map/all_gather | solution.py:40
  269.1 62.2 %all-gather.16.cloned.1.call-done = bf16[1,1,4096,1024]{2,3,1,0:T(8,128)(2,1)} async-done(((bf16[1,1,256,1024]{2,3,1,0:T(8,128)(2,1)}), bf16[1,1,4096,1024]{2,3,1,0:T(8,128)(2,1)}) %all-gather.16.cloned.1.call-update) | async-done | bytes 8388624 | tf_op jit(solution)/shard_map/all_gather | solution.py:41
  331.3 33.8 %conditional.3 = (f32[4,512,128]{2,1,0:T(8,128)}) conditional(s32[]{:T(128)} %convert_element_type.146, () %tuple.35, (bf16[4096,1024]{0,1:T(8,128)(2,1)}, s32[]{:T(128)}, bf16[4096,1024]{0,1:T(8,128)(2,1)}, s32[]{:T(128)}, s32[4096]{0:T(1024)S(1)}, /*index=5*/s32[1,512]{1,0:T(1,128)S(1)}, bf16[4,512,128]{1,2,0:T(8,128)(2,1)S(1)}) %tuple.107), branch_computations={%region_10.11_spmd, %region_11.14_spmd} | conditional | flops 1092620288 | bytes 19296452 | solution.py:64
  331.3 9.4 %constant_dynamic-slice_fusion.2 = (bf16[4096,512]{0,1:T(8,128)(2,1)}, bf16[4096,512]{0,1:T(8,128)(2,1)}) fusion(bf16[4096,1024]{0,1:T(8,128)(2,1)} %get-tuple-element.189, s32[]{:T(128)} %get-tuple-element.185, bf16[4096,1024]{0,1:T(8,128)(2,1)} %get-tuple-element.184), kind=kLoop, calls=%fused_computation.34 | loop fusion | bytes 16777220 | tf_op jit(solution)/shard_map/dynamic_slice | solution.py:45
  341.4 23.7 %while.33 = (s32[]{:T(128)}, f32[4,512,128]{2,1,0:T(8,128)}, bf16[4,512,128]{1,2,0:T(8,128)(2,1)S(1)}, bf16[4,4096,128]{1,2,0:T(8,128)(2,1)}, bf16[4,4096,128]{1...) while((s32[]{:T(128)}, f32[4,512,128]{2,1,0:T(8,128)}, ...), condition=%wide.region_13.13_spmd.clone, body=%wide.region_12.12_spmd.clone.sunk | while | flops 1092616192 | bytes 2515045 | solution.py:62
  341.4 5.9 %fusion.82 = f32[4,512,128]{2,1,0:T(8,128)} fusion(f32[4,512,128]{2,1,0:T(8,128)} %get-tuple-element.419, s32[]{:T(128)S(6)} %copy.42, s32[4096]{0:T(1024)S(1)} %get-tuple-element.433, s32[512]{0:T(512)S(1)} %get-tuple-element.432, pred[4096]{0:T(1024)(128)(4,1)S(1)} %get-tuple-element.434, bf16[4,4096,128]{1,2,0:T(8,128)(2,1)} %get-tuple-element.431, ...), kind=kOutput, calls=%fused_computation.22.clone.1 | convolution fusion | flops 1092616192 | bytes 2514944 | tf_op jit(solution)/shard_map/cond/branch_1_fun/while/body/eval_jaxpr/dot_general | solution.py:60
  347.4 5.9 %fusion.82 = f32[4,512,128]{2,1,0:T(8,128)} fusion(f32[4,512,128]{2,1,0:T(8,128)} %get-tuple-element.419, s32[]{:T(128)S(6)} %copy.42, s32[4096]{0:T(1024)S(1)} %get-tuple-element.433, s32[512]{0:T(512)S(1)} %get-tuple-element.432, pred[4096]{0:T(1024)(128)(4,1)S(1)} %get-tuple-element.434, bf16[4,4096,128]{1,2,0:T(8,128)(2,1)} %get-tuple-element.431, ...), kind=kOutput, calls=%fused_computation.22.clone.1 | convolution fusion | flops 1092616192 | bytes 2514944 | tf_op jit(solution)/shard_map/cond/branch_1_fun/while/body/eval_jaxpr/dot_general | solution.py:60
  353.3 5.9 %fusion.82 = f32[4,512,128]{2,1,0:T(8,128)} fusion(f32[4,512,128]{2,1,0:T(8,128)} %get-tuple-element.419, s32[]{:T(128)S(6)} %copy.42, s32[4096]{0:T(1024)S(1)} %get-tuple-element.433, s32[512]{0:T(512)S(1)} %get-tuple-element.432, pred[4096]{0:T(1024)(128)(4,1)S(1)} %get-tuple-element.434, bf16[4,4096,128]{1,2,0:T(8,128)(2,1)} %get-tuple-element.431, ...), kind=kOutput, calls=%fused_computation.22.clone.1 | convolution fusion | flops 1092616192 | bytes 2514944 | tf_op jit(solution)/shard_map/cond/branch_1_fun/while/body/eval_jaxpr/dot_general | solution.py:60
  359.2 5.9 %fusion.82 = f32[4,512,128]{2,1,0:T(8,128)} fusion(f32[4,512,128]{2,1,0:T(8,128)} %get-tuple-element.419, s32[]{:T(128)S(6)} %copy.42, s32[4096]{0:T(1024)S(1)} %get-tuple-element.433, s32[512]{0:T(512)S(1)} %get-tuple-element.432, pred[4096]{0:T(1024)(128)(4,1)S(1)} %get-tuple-element.434, bf16[4,4096,128]{1,2,0:T(8,128)(2,1)} %get-tuple-element.431, ...), kind=kOutput, calls=%fused_computation.22.clone.1 | convolution fusion | flops 1092616192 | bytes 2514944 | tf_op jit(solution)/shard_map/cond/branch_1_fun/while/body/eval_jaxpr/dot_general | solution.py:60
  371.9 3.0 convolution_convert_fusion
  374.9 25.4 %all-reduce.5.cloned.1.call-done = bf16[512,1024]{1,0:T(8,128)(2,1)} async-done(((bf16[512,1024]{1,0:T(8,128)(2,1)}), bf16[512,1024]{1,0:T(8,128)(2,1)}) %all-reduce.5.cloned.1.call-update) | async-done | bytes 1048592 | tf_op jit(solution)/shard_map/psum | solution.py:81
  400.3 3.1 add_bitcast_fusion
  (59 shorter events, 31.8 us)
Async XLA Ops:
  6.5 3.2 copy-start.4
  6.5 67.6 %all-gather.10.cloned.1.call-start = ((), (), s32[]{:S(2)}) async-start(), calls=%async_computation.2 | async-start | bytes 8912896 | tf_op jit(solution)/shard_map/all_gather | solution.py:40
  9.7 126.8 %all-gather.12.cloned.1.call-start = ((), (), s32[]{:S(2)}) async-start(), calls=%async_computation.3 | async-start | bytes 8912896 | tf_op jit(solution)/shard_map/all_gather | solution.py:41
  11.7 193.8 %all-reduce.3.cloned.1.call-start = ((), (), s32[]{:S(2)}) async-start(), calls=%async_computation | async-start | bytes 2097152 | tf_op jit(solution)/shard_map/psum | solution.py:81
  18.8 1.4 copy-start
  30.7 5.8 %copy-start.5 = (s32[1,256]{1,0:T(1,128)S(1)}, s32[1,256]{1,0:T(1,128)}, u32[]{:S(2)}) copy-start(s32[1,256]{1,0:T(1,128)} %param.18) | copy-start | bytes 3076
  32.1 104.5 %copy-start.6 = (s32[1,512]{1,0:T(1,128)S(1)}, s32[1,512]{1,0:T(1,128)}, u32[]{:S(2)}) copy-start(s32[1,512]{1,0:T(1,128)} %param.17) | copy-start | bytes 6148
  177.1 3.1 copy-start.2
  177.1 4.2 %copy-start.3 = (bf16[1,1,256,1024]{3,2,1,0:T(8,128)(2,1)S(1)}, bf16[1,1,256,1024]{3,2,1,0:T(8,128)(2,1)}, u32[]{:S(2)}) copy-start(bf16[1,1,256,1024]{3,2,1,0:T(8,128)(2,1)} %get-tuple-element.307) | copy-start | bytes 1572868
  180.1 89.0 %all-gather.14.cloned.1.call-start = ((), (), s32[]{:S(2)}) async-start(), calls=%async_computation.4 | async-start | bytes 8912896 | tf_op jit(solution)/shard_map/all_gather | solution.py:40
  181.2 150.1 %all-gather.16.cloned.1.call-start = ((), (), s32[]{:S(2)}) async-start(), calls=%async_computation.5 | async-start | bytes 8912896 | tf_op jit(solution)/shard_map/all_gather | solution.py:41
  182.3 218.0 %all-reduce.5.cloned.1.call-start = ((), (), s32[]{:S(2)}) async-start(), calls=%async_computation.1 | async-start | bytes 2097152 | tf_op jit(solution)/shard_map/psum | solution.py:81
  371.8 28.5 %copy-start.1 = (bf16[512,1024]{1,0:T(8,128)(2,1)S(1)}, bf16[512,1024]{1,0:T(8,128)(2,1)}, u32[]{:S(2)}) copy-start(bf16[512,1024]{1,0:T(8,128)(2,1)} %all-reduce.3.cloned.1.call-done) | copy-start | bytes 3145732
Sparse Core Ops, SparseCore 0:
  9.8 64.2 all-gather.9
  75.7 60.7 all-gather.11
  180.3 25.2 all-reduce.2
  207.1 61.9 all-gather.13
  270.7 60.6 all-gather.15
  375.0 25.2 all-reduce.4
where the time goes:
time: 411 us; the launch traced here: 410 us
  waiting for transfers between devices  225 us (55%)
  matrix products  65.7 us (16%)
  local copies, waits for them, and re-layouts  59.6 us (15%)
  blocking collectives  26.5 us (6%)
  other arithmetic  18.4 us (4%)
  between operations  14.3 us (3%)
    all_gather x2, waiting for transfers between devices, on_device(): lax.all_gather(hist_values[0, layer], ('cand', 'tensor'), axis=0, tiled=T...  125 us
    all_gather x2, waiting for transfers between devices, on_device(): lax.all_gather(hist_keys[0, layer], ('cand', 'tensor'), axis=0, tiled=True)  57.9 us
    dot_general x8, matrix products, one_head(): return jnp.dot(weights, value_one, preferred_element_type=jnp.float32)  47.4 us
    psum x2, waiting for transfers between devices, on_device(): lax.psum(partial_value.astype(jnp.bfloat16), 'tensor').astype(jnp.float32)  42.8 us
    all_gather x1, blocking collectives, on_device(): items = lax.all_gather(hist_ids[0], ('cand', 'tensor'), axis=0, tiled=True)  21.6 us
    dynamic_slice x2, local copies, waits for them, and re-layouts, on_device(): values = lax.dynamic_slice_in_dim(values, column, local, 1)  18.8 us
    dot_general x2, matrix products, on_device(): jnp.dot(normed, w_in[layer].reshape(width, 4 * local), preferred_element_...  12.1 us
    unnamed x20, local copies, waits for them, and re-layouts  11 us
  transfers between devices with their start and end apart: 6, of which 6 were waited for; matrix products, arithmetic and copies ran while one was open for 13% of the time, Pallas kernels for 0%

commit v1 on v0

--- a/solution.py
+++ b/solution.py
@@ -78,7 +78,9 @@
         squares = lax.psum(jnp.sum(product * product, axis=1), "tensor")
         normed_z = (product * lax.rsqrt(squares / width + 1e-06)[:, None]).astype(jnp.bfloat16)
         partial_value = jnp.dot(normed_z, w_out[layer], preferred_element_type=jnp.float32)
-        state = state + lax.psum(partial_value.astype(jnp.bfloat16), "tensor").astype(jnp.float32)
+        state = state + jax.lax.all_gather(partial_value.astype(jnp.bfloat16), "tensor").sum(
+            axis=0
+        ).astype(jnp.float32)
         if layer + 1 < LAYERS:
             normed = row_norm(state).astype(jnp.bfloat16)
     return state[None]

time: 411 us -> 390 us (0.949)
  waiting for transfers between devices: 225 us -> 200 us
    psum x2 -> x0, waiting for transfers between devices: 42.8 us -> none  [on_device(): lax.psum(partial_value.astype(jnp.bfloat16), 'tensor').astype(jnp.float32)]
    all_gather x0 -> x2, waiting for transfers between devices: none -> 19 us  [on_device(): jax.lax.all_gather(partial_value.astype(jnp.bfloat16), 'tensor').sum(axis=0)]
    reduce_sum x0 -> x2, other arithmetic: none -> 4.31 us  [on_device(): jax.lax.all_gather(partial_value.astype(jnp.bfloat16), 'tensor').sum(axis=0)]
  transfers between devices with their start and end apart: 6 -> 6, of which waited for: 6 -> 6; matrix products, arithmetic and copies ran while one was open for 13% -> 14% of each run, Pallas kernels for 0% -> 0%
where the time goes in v1:
time: 390 us; the launch traced here: 389 us
  waiting for transfers between devices  200 us (51%)
  matrix products  65.4 us (17%)
  local copies, waits for them, and re-layouts  61.5 us (16%)
  blocking collectives  26.5 us (7%)
  other arithmetic  20.9 us (5%)
  between operations  14.3 us (4%)
    all_gather x2, waiting for transfers between devices, on_device(): lax.all_gather(hist_values[0, layer], ('cand', 'tensor'), axis=0, tiled=T...  125 us
    all_gather x2, waiting for transfers between devices, on_device(): lax.all_gather(hist_keys[0, layer], ('cand', 'tensor'), axis=0, tiled=True)  56.2 us
    dot_general x8, matrix products, one_head(): return jnp.dot(weights, value_one, preferred_element_type=jnp.float32)  47.6 us
    all_gather x1, blocking collectives, on_device(): items = lax.all_gather(hist_ids[0], ('cand', 'tensor'), axis=0, tiled=True)  21.6 us
    all_gather x2, waiting for transfers between devices, on_device(): jax.lax.all_gather(partial_value.astype(jnp.bfloat16), 'tensor').sum(axis=0)  19 us
    dynamic_slice x2, local copies, waits for them, and re-layouts, on_device(): values = lax.dynamic_slice_in_dim(values, column, local, 1)  18.8 us
    unnamed x20, local copies, waits for them, and re-layouts  11.9 us
    dot_general x2, matrix products, on_device(): jnp.dot(normed, w_in[layer].reshape(width, 4 * local), preferred_element_...  11.9 us
  transfers between devices with their start and end apart: 6, of which 6 were waited for; matrix products, arithmetic and copies ran while one was open for 14% of the time, Pallas kernels for 0%

profile of v1, /device:TPU:1, one launch (start us, length us, event | category | flops | bytes accessed | tf_op | source)
XLA Modules:
  0.0 388.9 jit_solution(12853186851614032077)
XLA Ops:
  11.8 7.0 %fusion.68 = (bf16[1,1024,4,512]{3,2,1,0:T(4,128)(2,1)}, bf16[1,1024,4,512]{3,2,1,0:T(4,128)(2,1)S(1)}) fusion(bf16[2,1024,4,512]{3,2,1,0:T(4,128)(2,1)} %param.22), kind=kLoop, calls=%fused_computation.82 | loop fusion | bytes 16777216 | tf_op jit(solution)/shard_map/slice | solution.py:30
  20.5 4.9 %divide_multiply_fusion.1 = f32[512,2048]{1,0:T(8,128)} fusion(bf16[1024,2048]{1,0:T(8,128)(2,1)S(1)} %bitcast.180, bf16[1,512,1024]{2,1,0:T(8,128)(2,1)S(1)} %copy-done, f32[512]{0:T(512)S(1)} %add_rsqrt_fusion.3), kind=kOutput, calls=%fused_computation.37 | convolution fusion | flops 2153250816 | bytes 9439232 | tf_op jit(solution)/shard_map/dot_general | solution.py:29
  25.4 5.4 %copy.25 = f32[512,2048]{0,1:T(8,128)} copy(f32[512,2048]{1,0:T(8,128)} %divide_multiply_fusion.1) | data formatting | bytes 8388608 | tf_op jit(solution)/shard_map/reshape | solution.py:33
  32.1 3.8 convert.19
  36.6 21.6 %all-gather.2 = s32[1,4096]{1,0:T(1,128)S(1)} all-gather(s32[1,256]{1,0:T(1,128)S(1)} %copy-done.5), channel_id=4, replica_groups=mesh['user'=8,'cand'=8,'tensor'=2] {'cand','tensor'}, dimensions={1}, use_global_device_ids=true | all-gather | bytes 17408 | tf_op jit(solution)/shard_map/all_gather | solution.py:42
  60.6 13.5 %all-gather.14.cloned.1.call-done = bf16[1,1,4096,1024]{2,3,1,0:T(8,128)(2,1)} async-done(((bf16[1,1,256,1024]{2,3,1,0:T(8,128)(2,1)}), bf16[1,1,4096,1024]{2,3,1,0:T(8,128)(2,1)}) %all-gather.14.cloned.1.call-update) | async-done | bytes 8388624 | tf_op jit(solution)/shard_map/all_gather | solution.py:40
  74.1 62.4 %all-gather.16.cloned.1.call-done = bf16[1,1,4096,1024]{2,3,1,0:T(8,128)(2,1)} async-done(((bf16[1,1,256,1024]{2,3,1,0:T(8,128)(2,1)}), bf16[1,1,4096,1024]{2,3,1,0:T(8,128)(2,1)}) %all-gather.16.cloned.1.call-update) | async-done | bytes 8388624 | tf_op jit(solution)/shard_map/all_gather | solution.py:41
  136.5 33.8 %conditional.2 = (f32[4,512,128]{2,1,0:T(8,128)}) conditional(s32[]{:T(128)} %convert_element_type.177, () %tuple.33, (bf16[4096,1024]{0,1:T(8,128)(2,1)}, s32[]{:T(128)}, bf16[4096,1024]{0,1:T(8,128)(2,1)}, s32[]{:T(128)}, s32[4096]{0:T(1024)S(1)}, /*index=5*/s32[1,512]{1,0:T(1,128)S(1)}, bf16[4,512,128]{1,2,0:T(8,128)(2,1)S(1)}) %tuple.106), branch_computations={%region_1.2_spmd, %region_2.5_spmd} | conditional | flops 1092620288 | bytes 19296452 | solution.py:64
  136.5 9.4 %constant_dynamic-slice_fusion = (bf16[4096,512]{0,1:T(8,128)(2,1)}, bf16[4096,512]{0,1:T(8,128)(2,1)}) fusion(bf16[4096,1024]{0,1:T(8,128)(2,1)} %get-tuple-element.174, s32[]{:T(128)} %get-tuple-element.170, bf16[4096,1024]{0,1:T(8,128)(2,1)} %get-tuple-element.169), kind=kLoop, calls=%fused_computation.17 | loop fusion | bytes 16777220 | tf_op jit(solution)/shard_map/dynamic_slice | solution.py:45
  146.6 23.7 %while.32 = (s32[]{:T(128)}, f32[4,512,128]{2,1,0:T(8,128)}, bf16[4,512,128]{1,2,0:T(8,128)(2,1)S(1)}, bf16[4,4096,128]{1,2,0:T(8,128)(2,1)}, bf16[4,4096,128]{1...) while((s32[]{:T(128)}, f32[4,512,128]{2,1,0:T(8,128)}, ...), condition=%wide.region_4.4_spmd.clone, body=%wide.region_3.3_spmd.clone.sunk | while | flops 1092616192 | bytes 2515045 | solution.py:62
  146.6 5.9 %fusion.92 = f32[4,512,128]{2,1,0:T(8,128)} fusion(f32[4,512,128]{2,1,0:T(8,128)} %get-tuple-element.446, s32[]{:T(128)S(6)} %copy.49, s32[4096]{0:T(1024)S(1)} %get-tuple-element.460, s32[512]{0:T(512)S(1)} %get-tuple-element.459, pred[4096]{0:T(1024)(128)(4,1)S(1)} %get-tuple-element.461, bf16[4,4096,128]{1,2,0:T(8,128)(2,1)} %get-tuple-element.458, ...), kind=kOutput, calls=%fused_computation.5.clone.1 | convolution fusion | flops 1092616192 | bytes 2514944 | tf_op jit(solution)/shard_map/cond/branch_1_fun/while/body/eval_jaxpr/dot_general | solution.py:60
  152.6 5.9 %fusion.92 = f32[4,512,128]{2,1,0:T(8,128)} fusion(f32[4,512,128]{2,1,0:T(8,128)} %get-tuple-element.446, s32[]{:T(128)S(6)} %copy.49, s32[4096]{0:T(1024)S(1)} %get-tuple-element.460, s32[512]{0:T(512)S(1)} %get-tuple-element.459, pred[4096]{0:T(1024)(128)(4,1)S(1)} %get-tuple-element.461, bf16[4,4096,128]{1,2,0:T(8,128)(2,1)} %get-tuple-element.458, ...), kind=kOutput, calls=%fused_computation.5.clone.1 | convolution fusion | flops 1092616192 | bytes 2514944 | tf_op jit(solution)/shard_map/cond/branch_1_fun/while/body/eval_jaxpr/dot_general | solution.py:60
  158.5 5.9 %fusion.92 = f32[4,512,128]{2,1,0:T(8,128)} fusion(f32[4,512,128]{2,1,0:T(8,128)} %get-tuple-element.446, s32[]{:T(128)S(6)} %copy.49, s32[4096]{0:T(1024)S(1)} %get-tuple-element.460, s32[512]{0:T(512)S(1)} %get-tuple-element.459, pred[4096]{0:T(1024)(128)(4,1)S(1)} %get-tuple-element.461, bf16[4,4096,128]{1,2,0:T(8,128)(2,1)} %get-tuple-element.458, ...), kind=kOutput, calls=%fused_computation.5.clone.1 | convolution fusion | flops 1092616192 | bytes 2514944 | tf_op jit(solution)/shard_map/cond/branch_1_fun/while/body/eval_jaxpr/dot_general | solution.py:60
  164.4 5.9 %fusion.92 = f32[4,512,128]{2,1,0:T(8,128)} fusion(f32[4,512,128]{2,1,0:T(8,128)} %get-tuple-element.446, s32[]{:T(128)S(6)} %copy.49, s32[4096]{0:T(1024)S(1)} %get-tuple-element.460, s32[512]{0:T(512)S(1)} %get-tuple-element.459, pred[4096]{0:T(1024)(128)(4,1)S(1)} %get-tuple-element.461, bf16[4,4096,128]{1,2,0:T(8,128)(2,1)} %get-tuple-element.458, ...), kind=kOutput, calls=%fused_computation.5.clone.1 | convolution fusion | flops 1092616192 | bytes 2514944 | tf_op jit(solution)/shard_map/cond/branch_1_fun/while/body/eval_jaxpr/dot_general | solution.py:60
  177.1 3.0 convolution_convert_fusion.1
  182.6 5.6 %copy.38 = bf16[128,8,4,512]{3,1,2,0:T(8,128)(2,1)} copy(bf16[128,8,4,512]{3,2,1,0:T(4,128)(2,1)} %bitcast.165) | data formatting | bytes 8388608
  188.2 5.5 %all-gather.18.cloned.1.call-done = bf16[1024,1024]{1,0:T(8,128)(2,1)} async-done(((bf16[512,1024]{1,0:T(8,128)(2,1)}), bf16[1024,1024]{1,0:T(8,128)(2,1)}) %all-gather.18.cloned.1.call-update) | async-done | bytes 2097168 | tf_op jit(solution)/shard_map/all_gather | solution.py:81
  196.2 7.0 %divide_multiply_fusion = f32[512,2048]{1,0:T(8,128)} fusion(bf16[1024,2048]{1,0:T(8,128)(2,1)} %bitcast.179, bf16[512,1024]{1,0:T(8,128)(2,1)S(1)} %reduce_sum.81, bf16[1,512,1024]{2,1,0:T(8,128)(2,1)S(1)} %copy-done, f32[512]{0:T(512)S(1)} %add_rsqrt_fusion.1), kind=kOutput, calls=%fused_computation.36 | convolution fusion | flops 2154299392 | bytes 10487808 | tf_op jit(solution)/shard_map/dot_general | solution.py:29
  203.2 5.4 %copy.26 = f32[512,2048]{0,1:T(8,128)} copy(f32[512,2048]{1,0:T(8,128)} %divide_multiply_fusion) | data formatting | bytes 8388608 | tf_op jit(solution)/shard_map/reshape | solution.py:33
  214.3 42.8 %all-gather.20.cloned.1.call-done = bf16[1,1,4096,1024]{2,3,1,0:T(8,128)(2,1)} async-done(((bf16[1,1,256,1024]{2,3,1,0:T(8,128)(2,1)}), bf16[1,1,4096,1024]{2,3,1,0:T(8,128)(2,1)}) %all-gather.20.cloned.1.call-update) | async-done | bytes 8388624 | tf_op jit(solution)/shard_map/all_gather | solution.py:40
  257.1 62.1 %all-gather.22.cloned.1.call-done = bf16[1,1,4096,1024]{2,3,1,0:T(8,128)(2,1)} async-done(((bf16[1,1,256,1024]{2,3,1,0:T(8,128)(2,1)}), bf16[1,1,4096,1024]{2,3,1,0:T(8,128)(2,1)}) %all-gather.22.cloned.1.call-update) | async-done | bytes 8388624 | tf_op jit(solution)/shard_map/all_gather | solution.py:41
  319.2 33.9 %conditional.3 = (f32[4,512,128]{2,1,0:T(8,128)}) conditional(s32[]{:T(128)} %convert_element_type.177, () %tuple.35, (bf16[4096,1024]{0,1:T(8,128)(2,1)}, s32[]{:T(128)}, bf16[4096,1024]{0,1:T(8,128)(2,1)}, s32[]{:T(128)}, s32[4096]{0:T(1024)S(1)}, /*index=5*/s32[1,512]{1,0:T(1,128)S(1)}, bf16[4,512,128]{1,2,0:T(8,128)(2,1)}) %tuple.107), branch_computations={%region_10.11_spmd, %region_11.14_spmd} | conditional | flops 1092620288 | bytes 19296452 | solution.py:64
  319.2 9.4 %constant_dynamic-slice_fusion.2 = (bf16[4096,512]{0,1:T(8,128)(2,1)}, bf16[4096,512]{0,1:T(8,128)(2,1)}) fusion(bf16[4096,1024]{0,1:T(8,128)(2,1)} %get-tuple-element.189, s32[]{:T(128)} %get-tuple-element.185, bf16[4096,1024]{0,1:T(8,128)(2,1)} %get-tuple-element.184), kind=kLoop, calls=%fused_computation.34 | loop fusion | bytes 16777220 | tf_op jit(solution)/shard_map/dynamic_slice | solution.py:45
  329.3 23.9 %while.33 = (s32[]{:T(128)}, f32[4,512,128]{2,1,0:T(8,128)}, bf16[4,512,128]{1,2,0:T(8,128)(2,1)}, bf16[4,4096,128]{1,2,0:T(8,128)(2,1)}, bf16[4,4096,128]{1,2,0...) while((s32[]{:T(128)}, f32[4,512,128]{2,1,0:T(8,128)}, ...), condition=%wide.region_13.13_spmd.clone, body=%wide.region_12.12_spmd.clone.sunk | while | flops 1092616192 | bytes 2515045 | solution.py:62
  329.3 6.0 %fusion.88 = f32[4,512,128]{2,1,0:T(8,128)} fusion(f32[4,512,128]{2,1,0:T(8,128)} %get-tuple-element.419, s32[]{:T(128)S(6)} %copy.42, s32[4096]{0:T(1024)S(1)} %get-tuple-element.433, s32[512]{0:T(512)S(1)} %get-tuple-element.432, pred[4096]{0:T(1024)(128)(4,1)S(1)} %get-tuple-element.434, bf16[4,4096,128]{1,2,0:T(8,128)(2,1)} %get-tuple-element.431, ...), kind=kOutput, calls=%fused_computation.22.clone.1 | convolution fusion | flops 1092616192 | bytes 2514944 | tf_op jit(solution)/shard_map/cond/branch_1_fun/while/body/eval_jaxpr/dot_general | solution.py:60
  335.3 6.0 %fusion.88 = f32[4,512,128]{2,1,0:T(8,128)} fusion(f32[4,512,128]{2,1,0:T(8,128)} %get-tuple-element.419, s32[]{:T(128)S(6)} %copy.42, s32[4096]{0:T(1024)S(1)} %get-tuple-element.433, s32[512]{0:T(512)S(1)} %get-tuple-element.432, pred[4096]{0:T(1024)(128)(4,1)S(1)} %get-tuple-element.434, bf16[4,4096,128]{1,2,0:T(8,128)(2,1)} %get-tuple-element.431, ...), kind=kOutput, calls=%fused_computation.22.clone.1 | convolution fusion | flops 1092616192 | bytes 2514944 | tf_op jit(solution)/shard_map/cond/branch_1_fun/while/body/eval_jaxpr/dot_general | solution.py:60
  341.3 6.0 %fusion.88 = f32[4,512,128]{2,1,0:T(8,128)} fusion(f32[4,512,128]{2,1,0:T(8,128)} %get-tuple-element.419, s32[]{:T(128)S(6)} %copy.42, s32[4096]{0:T(1024)S(1)} %get-tuple-element.433, s32[512]{0:T(512)S(1)} %get-tuple-element.432, pred[4096]{0:T(1024)(128)(4,1)S(1)} %get-tuple-element.434, bf16[4,4096,128]{1,2,0:T(8,128)(2,1)} %get-tuple-element.431, ...), kind=kOutput, calls=%fused_computation.22.clone.1 | convolution fusion | flops 1092616192 | bytes 2514944 | tf_op jit(solution)/shard_map/cond/branch_1_fun/while/body/eval_jaxpr/dot_general | solution.py:60
  347.2 6.0 %fusion.88 = f32[4,512,128]{2,1,0:T(8,128)} fusion(f32[4,512,128]{2,1,0:T(8,128)} %get-tuple-element.419, s32[]{:T(128)S(6)} %copy.42, s32[4096]{0:T(1024)S(1)} %get-tuple-element.433, s32[512]{0:T(512)S(1)} %get-tuple-element.432, pred[4096]{0:T(1024)(128)(4,1)S(1)} %get-tuple-element.434, bf16[4,4096,128]{1,2,0:T(8,128)(2,1)} %get-tuple-element.431, ...), kind=kOutput, calls=%fused_computation.22.clone.1 | convolution fusion | flops 1092616192 | bytes 2514944 | tf_op jit(solution)/shard_map/cond/branch_1_fun/while/body/eval_jaxpr/dot_general | solution.py:60
  353.2 2.5 copy.23
  357.3 2.5 psum.15
  361.5 2.9 convolution_convert_fusion
  364.5 13.5 %all-gather.24.cloned.1.call-done = bf16[1024,1024]{1,0:T(8,128)(2,1)} async-done(((bf16[512,1024]{1,0:T(8,128)(2,1)}), bf16[1024,1024]{1,0:T(8,128)(2,1)}) %all-gather.24.cloned.1.call-update) | async-done | bytes 2097168 | tf_op jit(solution)/shard_map/all_gather | solution.py:81
  (61 shorter events, 36.8 us)
Async XLA Ops:
  6.5 3.2 copy-start.4
  6.5 67.5 %all-gather.14.cloned.1.call-start = ((), (), s32[]{:S(2)}) async-start(), calls=%async_computation | async-start | bytes 8912896 | tf_op jit(solution)/shard_map/all_gather | solution.py:40
  9.7 126.8 %all-gather.16.cloned.1.call-start = ((), (), s32[]{:S(2)}) async-start(), calls=%async_computation.1 | async-start | bytes 8912896 | tf_op jit(solution)/shard_map/all_gather | solution.py:41
  11.7 181.9 %all-gather.18.cloned.1.call-start = ((), (), s32[]{:S(2)}) async-start(), calls=%async_computation.2 | async-start | bytes 3145728 | tf_op jit(solution)/shard_map/all_gather | solution.py:81
  18.8 1.4 copy-start
  30.7 5.8 %copy-start.5 = (s32[1,256]{1,0:T(1,128)S(1)}, s32[1,256]{1,0:T(1,128)}, u32[]{:S(2)}) copy-start(s32[1,256]{1,0:T(1,128)} %param.18) | copy-start | bytes 3076
  32.1 104.5 %copy-start.6 = (s32[1,512]{1,0:T(1,128)S(1)}, s32[1,512]{1,0:T(1,128)}, u32[]{:S(2)}) copy-start(s32[1,512]{1,0:T(1,128)} %param.17) | copy-start | bytes 6148
  177.1 3.1 copy-start.1
  177.1 4.2 %copy-start.2 = (bf16[1,1,256,1024]{3,2,1,0:T(8,128)(2,1)S(1)}, bf16[1,1,256,1024]{3,2,1,0:T(8,128)(2,1)}, u32[]{:S(2)}) copy-start(bf16[1,1,256,1024]{3,2,1,0:T(8,128)(2,1)} %get-tuple-element.307) | copy-start | bytes 1572868
  180.1 77.0 %all-gather.20.cloned.1.call-start = ((), (), s32[]{:S(2)}) async-start(), calls=%async_computation.3 | async-start | bytes 8912896 | tf_op jit(solution)/shard_map/all_gather | solution.py:40
  181.3 138.0 %all-gather.22.cloned.1.call-start = ((), (), s32[]{:S(2)}) async-start(), calls=%async_computation.4 | async-start | bytes 8912896 | tf_op jit(solution)/shard_map/all_gather | solution.py:41
  182.3 195.7 %all-gather.24.cloned.1.call-start = ((), (), s32[]{:S(2)}) async-start(), calls=%async_computation.5 | async-start | bytes 3145728 | tf_op jit(solution)/shard_map/all_gather | solution.py:81
  213.3 0.8 copy-start.3
Sparse Core Ops, SparseCore 0:
  9.8 64.1 all-gather.13
  75.7 60.7 all-gather.15
  180.3 13.3 all-gather.17
  195.1 61.9 all-gather.19
  258.6 60.6 all-gather.21
  364.6 13.3 all-gather.23
